TPU v7x, 32 devices: a whole 2x2x4 slice. The times are simulated.
32 devices in a mesh: slide: 2 (over y), seq: 16 (over z, x, core), head: 1.
Axes of the slice: x: 2, y: 2, z: 4, core: 2. Of those that a mesh axis runs over, the one named last changes fastest.
Arguments:
- queries: bfloat16 [16384, 768], P(('slide', 'seq'), 'head'), parts along dimension 0, may hold values from -14 to 14
- key_states: bfloat16 [16384, 768], P(('slide', 'seq'), 'head'), parts along dimension 0, may hold values from -4 to 4
- value_states: bfloat16 [16384, 768], P(('slide', 'seq'), 'head'), parts along dimension 0, may hold values from -6 to 6
- offsets_mid: int32 [16], replicated, may hold values from 0 to 3
- offsets_top: int32 [16], replicated, may hold values from 0 to 3
- out_weight: bfloat16 [768, 768], P('head'), may hold values from -0.21875 to 0.21875
Outputs:
- projected: bfloat16 [16384, 768], P(('slide', 'seq', 'head')), parts along dimension 0
There are 2 independent parts, one for each index of `slide`. A program takes and returns all parts, laid end to end along the dimension named above; an argument that names none is the same for every part. Nothing has to cross between parts.
All inputs are finite; a program needn't handle non-finite values.
Results may differ from a plain program's by a relative error of at most 0.0052.
Values may be sent and summed in bfloat16 or wider, within the bound.
No kernel may reach another device: no remote copies, remote signals or barrier semaphores. Data moves between devices by JAX's collectives and lax.ppermute only.
A program may use at most 64 MiB of HBM per device.

v0:
```python
import functools

import jax
import jax.numpy as jnp
from jax import lax
from jax.experimental import pallas as pl
from jax.experimental.pallas import tpu as pltpu
from jax.sharding import PartitionSpec as P

SEG = 2048
LOG2E = 1.4426950408889634
VMEM_LIMIT = 40 * 1024 * 1024
VMEM_MOST = 60 * 1024 * 1024
BF16 = jnp.bfloat16
F32 = jnp.float32


def partner_2(block, axis, apart):
    count = lax.axis_size(axis)
    route = []
    for low in range(count):
        high = low | 1 << apart
        if high != low and high < count:
            route += [(low, high), (high, low)]
    return lax.ppermute(block, axis, route)


def attend_head(triple_in):
    query_rows, key_rows, value_rows = triple_in
    score_scale = query_rows.shape[-1] ** (-0.5)
    scores = jnp.dot(query_rows, key_rows.T, preferred_element_type=jnp.float32) * score_scale
    row_max = jnp.max(scores, axis=1)
    shifted = jnp.exp(scores - row_max[:, None])
    row_total = jnp.sum(shifted, axis=1)
    weights = shifted.astype(jnp.bfloat16)
    numerator = jnp.dot(weights, value_rows, preferred_element_type=jnp.float32)
    return (numerator, row_total, row_max)


def attend_local(query_rows, pair_rows):
    return lax.map(
        attend_head,
        (
            query_rows.transpose(1, 0, 2),
            pair_rows[:, 0].transpose(1, 0, 2),
            pair_rows[:, 1].transpose(1, 0, 2),
        ),
    )


def pick_rows(states, offsets, rate):
    row_count, inner_count, heads_here, head_width = states.shape
    picker = (jnp.arange(rate)[:, None] == offsets[None, :]).astype(jnp.bfloat16)
    folded = states.reshape(row_count // rate, rate, inner_count, heads_here, head_width)
    return jnp.einsum("archd,rh->achd", folded, picker, preferred_element_type=jnp.float32).astype(
        jnp.bfloat16
    )


def spread_back(numerator, row_total, row_max, offsets, rate):
    heads_here, picked_count, head_width = numerator.shape
    chosen = jnp.arange(rate)[:, None] == offsets[None, :]
    full_num = jnp.where(chosen[None, :, :, None], numerator.transpose(1, 0, 2)[:, None], 0.0)
    full_total = jnp.where(chosen[None], row_total.T[:, None], 0.0)
    full_max = jnp.where(chosen[None], row_max.T[:, None], -1e30)
    return (
        full_num.reshape(picked_count * rate, heads_here, head_width),
        full_total.reshape(picked_count * rate, heads_here),
        full_max.reshape(picked_count * rate, heads_here),
    )


def doubling(buffer, steps_count):
    position = lax.axis_index("seq")
    for bit_index in range(steps_count):
        partner = partner_2(buffer, "seq", bit_index)
        is_lower = position >> bit_index & 1 == 0
        buffer = jnp.where(
            is_lower, jnp.concatenate([buffer, partner], 0), jnp.concatenate([partner, buffer], 0)
        )
    return buffer


def shards_general(queries, key_states, value_states, offsets_mid, offsets_top, out_weight):
    tok_rows = queries.shape[0]
    heads_local = offsets_mid.shape[0] // lax.axis_size("head")
    head_size = queries.shape[1] // heads_local
    seq_devices = lax.axis_size("seq")
    seq_total = tok_rows * seq_devices
    width_mid = min(16 * SEG, seq_total)
    rate_mid = width_mid // SEG
    rate_top = seq_total // SEG
    start_head = lax.axis_index("head") * heads_local
    mid_local = lax.dynamic_slice(offsets_mid, (start_head,), (heads_local,))
    top_local = lax.dynamic_slice(offsets_top, (start_head,), (heads_local,))
    query_heads = queries.reshape(tok_rows, 1, heads_local, head_size)
    paired = jnp.stack([key_states, value_states], axis=1).reshape(
        tok_rows, 2, heads_local, head_size
    )
    near_bits = (SEG // tok_rows).bit_length() - 1
    near_rows = doubling(paired.reshape(tok_rows, -1), near_bits).reshape(
        SEG, 2, heads_local, head_size
    )
    near_num, near_total, near_max = attend_local(query_heads[:, 0], near_rows)
    level_near = spread_back(
        near_num, near_total, near_max, jnp.zeros((heads_local,), jnp.int32), 1
    )
    mid_q = pick_rows(query_heads, mid_local, rate_mid)[:, 0]
    mid_kv = pick_rows(paired, mid_local, rate_mid)
    mid_group = width_mid // tok_rows
    mid_bits = mid_group.bit_length() - 1
    mid_rows = doubling(mid_kv.reshape(mid_kv.shape[0], -1), mid_bits).reshape(
        SEG, 2, heads_local, head_size
    )
    mid_num, mid_total, mid_max = attend_local(mid_q, mid_rows)
    level_mid = spread_back(mid_num, mid_total, mid_max, mid_local, rate_mid)
    top_q = pick_rows(query_heads, top_local, rate_top)[:, 0]
    top_kv = pick_rows(paired, top_local, rate_top)
    top_rows = lax.all_gather(
        top_kv.reshape(top_kv.shape[0], -1), "seq", axis=0, tiled=True
    ).reshape(SEG, 2, heads_local, head_size)
    top_num, top_total, top_max = attend_local(top_q, top_rows)
    level_top = spread_back(top_num, top_total, top_max, top_local, rate_top)
    levels = [level_near, level_mid, level_top]
    overall = jnp.maximum(jnp.maximum(level_near[2], level_mid[2]), level_top[2])
    numerator = jnp.zeros((tok_rows, heads_local, head_size), jnp.float32)
    row_total = jnp.zeros((tok_rows, heads_local), jnp.float32)
    for level_num, level_total, level_max in levels:
        factor = jnp.exp(level_max - overall)
        numerator = numerator + factor[..., None] * level_num
        row_total = row_total + factor * level_total
    attention = (
        (numerator / row_total[..., None])
        .astype(jnp.bfloat16)
        .reshape(tok_rows, heads_local * head_size)
    )
    result = lax.psum_scatter(
        jnp.dot(attention, out_weight, preferred_element_type=jnp.float32),
        "head",
        scatter_dimension=0,
        tiled=True,
    )
    return result.astype(jnp.bfloat16)


RATE = 4
GROUP = 4
HG = 4
STEP = 2
DH = 48
BLK = 128
HALF = 2 * BLK
TOK = 512
DX = 64


def dot(a, b):
    return jnp.dot(a, b, preferred_element_type=F32)


def dot_nt(a, b):
    return lax.dot_general(a, b, (((1,), (1,)), ((), ())), preferred_element_type=F32)


def class_of_slots(off_mid, off_top):
    first = off_mid
    second = jnp.where(off_top == off_mid, lax.rem(off_mid + 1, RATE), off_top)
    free0 = (first != 0) & (second != 0)
    free1 = (first != 1) & (second != 1)
    third = jnp.where(free0, 0, jnp.where(free1, 1, 2))
    return first, second, third, 6 - first - second - third


def head_of(place, j, p):
    return ((place[0] & (GROUP - 1)) ^ j) * HG + ((place[0] // GROUP) ^ p)


def token_picker():
    row = lax.broadcasted_iota(jnp.int32, (TOK, TOK), 0)
    col = lax.broadcasted_iota(jnp.int32, (TOK, TOK), 1)
    return (col == RATE * (row % BLK) + row // BLK).astype(BF16)


def fill_class_major(block, picker, scratch):
    ordered = dot(picker, block).astype(BF16)
    step = 256
    eye = (
        lax.broadcasted_iota(jnp.int32, (step, step), 0)
        == lax.broadcasted_iota(jnp.int32, (step, step), 1)
    ).astype(BF16)
    for c in range(0, block.shape[1], step):
        scratch[c : c + step, :] = dot_nt(eye, ordered[:, c : c + step]).astype(BF16)


def lane_block(index):
    return pl.ds(pl.multiple_of(index * BLK, BLK), BLK)


def head_rows(head):
    return pl.ds(pl.multiple_of(head * DH, 16), DH)


def pack_kernel(place, mid, top, k_hbm, v_hbm, q_hbm, *refs):
    outs, refs = refs[:6], refs[6:]
    blocks, held, packed, sems_in, sems_out = refs[:3], refs[3:6], refs[6:12], refs[12], refs[13]
    loads = [
        pltpu.make_async_copy(hbm, block, sems_in.at[i])
        for i, (hbm, block) in enumerate(zip((k_hbm, v_hbm, q_hbm), blocks))
    ]
    for load in loads:
        load.start()
    picker = token_picker()
    stores = []
    for n, (load, block, scratch) in enumerate(zip(loads, blocks, held)):
        load.wait()
        fill_class_major(block[...], picker, scratch)
        rows = slice(n * DH, (n + 1) * DH)
        for i, (j, first, count) in enumerate(
            ((0, 0, 4), (1, 0, 4), (2, 0, 2), (3, 0, 2), (2, 2, 2), (3, 2, 2))
        ):
            for p in range(HG):
                head = head_of(place, j, p)
                slots = class_of_slots(mid[head], top[head])
                for s in range(count):
                    packed[i][p, rows, s * BLK : (s + 1) * BLK] = scratch[
                        head_rows(head), lane_block(slots[first + s])
                    ]
            store = pltpu.make_async_copy(
                packed[i].at[:, rows], outs[i].at[:, rows], sems_out.at[i, n]
            )
            store.start()
            stores.append(store)
    for store in stores:
        store.wait()


def regroup_kernel(a_ref, b_ref, *refs):
    for s, out in enumerate(refs[-3:]):
        out[0] = a_ref[s + 1, :, 0:HALF]
        out[1] = b_ref[s + 1, :, 0:HALF]


def split_query(q):
    scaled = q.astype(F32) * (DH**-0.5 * LOG2E)
    high = scaled.astype(BF16)
    low = (scaled - high.astype(F32)).astype(BF16)
    return jnp.concatenate([high, low], axis=0)


def twice_keys(keys_t):
    both = jnp.concatenate([keys_t, keys_t], axis=0).astype(F32)
    return both.T.astype(BF16)


def column_max(blocks):
    best = jnp.max(blocks[0], axis=0, keepdims=True)
    for block in blocks[1:]:
        best = jnp.maximum(best, jnp.max(block, axis=0, keepdims=True))
    return best


def near_kernel(inputs, units, tasks, carried, place, mid, top, *refs):
    pieces = dict(zip(inputs, refs[: len(inputs)]))
    refs = refs[len(inputs) :]
    old = [refs[2 * i : 2 * i + 2] for i in range(carried)]
    outs = refs[2 * carried : 2 * carried + 2 * len(tasks)]
    k_s, v_s = refs[-2:]
    v_s[:, DH:DX, :] = jnp.ones((STEP, DX - DH, v_s.shape[2]), BF16)
    lane_slot = lax.broadcasted_iota(jnp.int32, (1, HALF), 1) // BLK

    def lookup(j, slot):
        first = 0 if (j, 0) in pieces and pieces[j, 0].shape[2] > HALF else slot // 2 * 2
        return pieces[j, first], (slot - first) * BLK

    chunks = []
    row = 0
    for label, members in units:
        chunks.append((label, slice(row, row + len(members) * BLK)))
        row += len(members) * BLK
    members = [member for _, group in units for member in group]

    def prepare(h):
        head = head_of(place, 0, pl.program_id(0) * STEP + h)
        same = mid[head] == top[head]
        for i, (j, slot) in enumerate(members):
            ref, lane = lookup(j, slot)
            rows = slice(i * BLK, (i + 1) * BLK)
            k_s[h, rows, :] = twice_keys(ref[h, 0:DH, lane : lane + BLK])
            v_s[h, 0:DH, rows] = ref[h, DH : 2 * DH, lane : lane + BLK]
        return [
            jnp.where(lane_slot == 0, jnp.where(same, 1.584962500721156, 1.0), 0.0),
            jnp.where(lane_slot == 1, jnp.where(same, 0.0, 1.0), 0.0),
        ]

    flat = [
        (h, query, low, merge, out, i)
        for h in range(STEP)
        for out, group in enumerate(tasks)
        for i, (query, low, merge) in enumerate(group)
    ]

    def score(task):
        h, (j, half), low = task[:3]
        ref, lane = lookup(j, 2 * half)
        query = split_query(ref[h, 2 * DH :, lane : lane + HALF])
        return [dot(k_s[h, rows, :], query) for _, rows in chunks[low:]]

    again = [prepare(h) for h in range(STEP)]
    scores = score(flat[0])
    for n, (h, (_, half), low, merge, out, i) in enumerate(flat):
        following = score(flat[n + 1]) if n + 1 < len(flat) else None
        best = column_max(scores)
        if merge is not None:
            acc_in, max_in = old[merge[0]]
            old_max = max_in[h, merge[1], 0:1, :]
            best = jnp.maximum(best, old_max)
        acc = None
        for (label, rows), block in zip(chunks[low:], scores):
            shift = best if half == 1 or label is None else best - again[h][label]
            part = dot(v_s[h, :, rows], jnp.exp2(block - shift).astype(BF16))
            acc = part if acc is None else acc + part
        if merge is not None:
            acc = acc + acc_in[h, merge[1]] * jnp.exp2(old_max - best)
        acc_ref, max_ref = outs[2 * out : 2 * out + 2]
        acc_ref[h, i] = acc
        max_ref[h, i] = jnp.broadcast_to(best, (8, HALF))
        scores = following


def far_kernel(place, mid, top, *refs):
    own, beyond = refs[:GROUP], refs[GROUP : GROUP + 6]
    outs = refs[GROUP + 6 : GROUP + 6 + RATE]
    k_s, v_s = refs[GROUP + 6 + RATE :]
    head = head_of(place, 0, 0)
    same = mid[head] == top[head]
    slots = (0, jnp.where(same, 0, 1))

    def source(s, j):
        return own[j].at[0] if s == 0 else beyond[2 * (s - 1) + j // 2].at[j % 2]

    for level, slot in enumerate(slots):
        for s in range(RATE):
            for j in range(GROUP):
                here = slice(j * BLK, (j + 1) * BLK)
                ref = source(s, j)
                k_s[level, s, here, :] = twice_keys(ref[0:DH, lane_block(slot)])
                v_s[level, s, 0:DH, here] = ref[DH : 2 * DH, lane_block(slot)]
    v_s[:, :, DH:DX, :] = jnp.ones((2, RATE, DX - DH, TOK), BF16)
    row = lax.broadcasted_iota(jnp.int32, (16, HALF), 0)
    tasks = [(s, level, chip) for s in range(RATE) for level in range(2) for chip in range(2)]

    def score(task):
        s, level, chip = task
        query = jnp.concatenate(
            [
                split_query(source(s, 2 * chip + i)[2 * DH :, lane_block(slots[level])])
                for i in range(2)
            ],
            axis=1,
        )
        return [dot(k_s[level, b], query) for b in range(RATE) if b != s]

    scores = score(tasks[0])
    for n, (s, level, chip) in enumerate(tasks):
        following = score(tasks[n + 1]) if n + 1 < len(tasks) else None
        best = column_max(scores)
        acc = None
        for i, b in enumerate([b for b in range(RATE) if b != s]):
            part = dot(v_s[level, b], jnp.exp2(scores[i] - best).astype(BF16))
            acc = part if acc is None else acc + part
        total = acc[DH : DH + 1, :]
        result = (acc[0:DH, :] / total).astype(BF16)
        lse = best + jnp.log2(total)
        if level == 0:
            lse = jnp.where(same, lse + 1.0, lse)
        else:
            lse = jnp.where(same, -1e30, lse)
        high = lse.astype(BF16).astype(F32)
        middle = (lse - high).astype(BF16).astype(F32)
        low = lse - high - middle
        tail = jnp.where(row == 0, high, jnp.where(row == 1, middle, jnp.where(row == 2, low, 0.0)))
        tail = tail.astype(BF16)
        for i in range(2):
            start = (2 * chip + i) * HALF + level * BLK
            lanes = slice(start, start + BLK)
            outs[s][0:DH, lanes] = result[:, i * BLK : (i + 1) * BLK]
            outs[s][DH:DX, lanes] = tail[:, i * BLK : (i + 1) * BLK]
        scores = following


def combine_kernel(chip, acc_ref, max_ref, *refs):
    far, outs = refs[:HG], refs[HG:]
    for i in range(2):
        lanes = slice((2 * chip + i) * HALF, (2 * chip + i + 1) * HALF)
        for p in range(HG):
            acc, best = acc_ref[p, 2 * i], max_ref[p, 2 * i, 0:1, :]
            tail = far[p][DH:DX, lanes].astype(F32)
            lse = tail[0:1] + tail[1:2] + tail[2:3]
            overall = jnp.maximum(best, lse)
            near_factor, far_factor = jnp.exp2(best - overall), jnp.exp2(lse - overall)
            total = acc[DH : DH + 1] * near_factor + far_factor
            value = acc[0:DH] * near_factor + far[p][0:DH, lanes].astype(F32) * far_factor
            outs[i][p, :, 0:HALF] = (value / total).astype(BF16)
            acc = acc_ref[p, 2 * i + 1]
            outs[i][p, :, HALF:] = (acc[0:DH] / acc[DH : DH + 1]).astype(BF16)


def project_kernel(place, mid, top, *refs):
    parts = refs[:GROUP]
    w_ref, out_ref, held = refs[GROUP:]
    for j in range(GROUP):
        for p in range(HG):
            head = head_of(place, j, p)
            slots = class_of_slots(mid[head], top[head])
            for s in range(RATE):
                held[head_rows(head), lane_block(slots[s])] = parts[j][
                    p, :, s * BLK : (s + 1) * BLK
                ]
    row = lax.broadcasted_iota(jnp.int32, (TOK, TOK), 0)
    col = lax.broadcasted_iota(jnp.int32, (TOK, TOK), 1)
    picker = (row == RATE * (col % BLK) + col // BLK).astype(BF16)
    attention = dot_nt(picker, held[...]).astype(BF16)
    out_ref[...] = dot(attention, w_ref[...]).astype(BF16)


def whole(shape):
    return pl.BlockSpec(shape, lambda *_: (0,) * len(shape))


def per_head(shape):
    return pl.BlockSpec(shape, lambda h, *_: (h,) + (0,) * (len(shape) - 1))


def call(
    kernel, scalars, args, grid, in_specs, outs, scratch, scores,
    limit=VMEM_LIMIT, aliases={}, after=(),
):
    known = len(scalars) + len(args)

    def body(*refs):
        kernel(*refs[:known], *refs[known + len(after) :])

    return pl.pallas_call(
        body if after else kernel,
        grid_spec=pltpu.PrefetchScalarGridSpec(
            num_scalar_prefetch=len(scalars),
            grid=grid,
            in_specs=list(in_specs) + [pl.BlockSpec(memory_space=pl.ANY)] * len(after),
            out_specs=[spec for spec, _ in outs],
            scratch_shapes=scratch,
        ),
        out_shape=[shape for _, shape in outs],
        input_output_aliases=aliases,
        compiler_params=pltpu.CompilerParams(vmem_limit_bytes=limit),
        cost_estimate=pl.CostEstimate(flops=0, bytes_accessed=0, transcendentals=0),
    )(*scalars, *args, *after)


def within(array, apart):
    count = lax.axis_size("seq")
    return lax.ppermute(array, "seq", [(i, i ^ apart) for i in range(count)])


def across(array, segments):
    return within(array, GROUP * segments)


def shards_four(queries, key_states, value_states, offsets_mid, offsets_top, out_weight):
    width = queries.shape[1]
    place = lax.axis_index("seq").astype(jnp.int32).reshape(1)
    scalars = (place, offsets_mid, offsets_top)
    full = jax.ShapeDtypeStruct((HG, 3 * DH, TOK), BF16)
    piece = jax.ShapeDtypeStruct((HG, 3 * DH, HALF), BF16)
    pair = jax.ShapeDtypeStruct((2, 3 * DH, HALF), BF16)
    anywhere = pl.BlockSpec(memory_space=pl.ANY)
    shapes = [full] * 2 + [piece] * 4
    own0, own1, sel2, sel3, rest2, rest3 = call(
        pack_kernel, scalars, (key_states, value_states, queries), (1,),
        [anywhere] * 3,
        [(anywhere, shape) for shape in shapes],
        [pltpu.VMEM((TOK, width), BF16)] * 3
        + [pltpu.VMEM((width, TOK), BF16)] * 3
        + [pltpu.VMEM(shape.shape, BF16) for shape in shapes]
        + [pltpu.SemaphoreType.DMA((3,)), pltpu.SemaphoreType.DMA((6, 3))],
        1 << 19, VMEM_MOST,
    )
    own1 = within(own1, 1)
    sel2, sel3 = within(sel2, 2), within(sel3, 3)

    def regroup(a, b, through, after):
        shapes = [jax.ShapeDtypeStruct(x.shape, x.dtype) for x in through] + [pair] * 3
        return call(
            regroup_kernel, (), (a, b, *through), (1,),
            [whole(a.shape), whole(b.shape)] + [anywhere] * len(through),
            [(anywhere, x) for x in shapes[: len(through)]] + [(whole(pair.shape), pair)] * 3,
            [], 1 << 17,
            aliases={2 + i: i for i in range(len(through))}, after=after,
        )

    def state(count):
        return [
            (per_head((STEP, count, rows, HALF)), jax.ShapeDtypeStruct((HG, count, rows, HALF), F32))
            for rows in (DX, 8)
        ]

    def near(held, units, tasks, old, after=()):
        sizes = [len(members) * BLK for _, members in units]
        scores = sum(sum(sizes[low:]) * HALF for group in tasks for _, low, _ in group)
        return call(
            functools.partial(near_kernel, list(held), units, tasks, len(old)), scalars,
            (*held.values(), *[x for one in old for x in one]), (HG // STEP,),
            [per_head((STEP,) + x.shape[1:]) for x in held.values()]
            + [per_head((STEP,) + x.shape[1:]) for one in old for x in one],
            [out for group in tasks for out in state(len(group))],
            [
                pltpu.VMEM((STEP, sum(sizes), 2 * DH), BF16),
                pltpu.VMEM((STEP, DX, sum(sizes)), BF16),
            ],
            HG * scores, after=after,
        )

    def units_of(a, b):
        return [(0, [(a, 0), (b, 0)]), (1, [(a, 1), (b, 1)])], [
            (None, [(a, 2), (a, 3), (b, 2), (b, 3)])
        ]

    own_sel, own_rest = units_of(0, 1)
    other_sel, other_rest = units_of(2, 3)
    own = [(0, 0), (0, 1), (1, 0), (1, 1)]

    ours = regroup(own0, own1, (), ())
    ours = [across(x, s + 1) for s, x in enumerate(ours)]
    held = {(0, 0): own0, (1, 0): own1}
    state_own = near(held, own_sel + own_rest, [[(q, 0, None) for q in own]], [])
    rest2, rest3, *theirs = regroup(
        sel2, sel3, (rest2, rest3), (state_own[1], *ours)
    )
    theirs = [across(x, s + 1) for s, x in enumerate(theirs)]
    rest2, rest3 = within(rest2, 2), within(rest3, 3)
    beyond = [x for both in zip(ours, theirs) for x in both]

    held.update({(2, 0): sel2, (3, 0): sel3})
    out = near(
        held, own_sel + own_rest + other_sel,
        [
            [(q, 3, (0, i)) for i, q in enumerate(own)],
            [((2, 0), 0, None), ((3, 0), 0, None)],
        ],
        [state_own],
    )
    state_own, state_sel = out[:2], out[2:]

    result = jax.ShapeDtypeStruct((DX, GROUP * HALF), BF16)
    piece_0 = pl.BlockSpec((1, 3 * DH, HALF), lambda *_: (0, 0, 0))
    results = call(
        far_kernel, scalars, (own0, own1, sel2, sel3, *beyond), (1,),
        [piece_0] * GROUP + [whole(pair.shape)] * 6,
        [(whole(result.shape), result)] * RATE,
        [
            pltpu.VMEM((2, RATE, TOK, 2 * DH), BF16),
            pltpu.VMEM((2, RATE, DX, TOK), BF16),
        ],
        RATE * 2 * 3 * TOK * TOK, after=(out[1],),
    )
    back = [results[0]] + [across(results[s], s) for s in range(1, RATE)]

    held.update({(2, 2): rest2, (3, 2): rest3})
    units = own_sel + own_rest + other_sel + other_rest
    attended = jax.ShapeDtypeStruct((HG, DH, TOK), BF16)

    def combine(chip, state):
        return call(
            functools.partial(combine_kernel, chip), (), (*state, *back), (1,),
            [whole(x.shape) for x in state] + [whole(result.shape)] * HG,
            [(whole(attended.shape), attended)] * 2,
            [],
            1 << 18,
        )

    state_other = near(
        held, units,
        [
            [
                ((2, 0), 5, (0, 0)), ((2, 1), 0, None),
                ((3, 0), 5, (0, 1)), ((3, 1), 0, None),
            ]
        ],
        [state_sel],
        after=results[:1],
    )
    part2, part3 = combine(1, state_other)
    state_own = near(
        {(2, 2): rest2, (3, 2): rest3, **{q: held[q] for q in ((0, 0), (1, 0))}},
        other_rest,
        [[(q, 0, (0, i)) for i, q in enumerate(own)]],
        [state_own],
        after=(part2,),
    )
    part0, part1 = combine(0, state_own)
    parts = [part0, within(part1, 1), within(part2, 2), within(part3, 3)]
    return call(
        project_kernel, scalars, (*parts, out_weight), (1,),
        [whole(attended.shape)] * GROUP + [whole((width, width))],
        [(whole((TOK, width)), jax.ShapeDtypeStruct((TOK, width), BF16))],
        [pltpu.VMEM((width, TOK), BF16)],
        1 << 18,
    )[0]


def shards(queries, key_states, value_states, offsets_mid, offsets_top, out_weight):
    tokens, width = queries.shape
    heads = offsets_mid.shape[0]
    fits = (
        lax.axis_size("head") == 1
        and lax.axis_size("seq") == GROUP * RATE
        and tokens == TOK
        and heads == GROUP * HG
        and width == heads * DH
    )
    run = shards_four if fits else shards_general
    return run(queries, key_states, value_states, offsets_mid, offsets_top, out_weight)


def solution(mesh):
    in_specs = (
        P(("slide", "seq"), "head"),
        P(("slide", "seq"), "head"),
        P(("slide", "seq"), "head"),
        P(),
        P(),
        P("head", None),
    )
    out_specs = P(("slide", "seq", "head"), None)
    return jax.shard_map(shards, mesh=mesh, in_specs=in_specs, out_specs=out_specs, check_vma=False)
```

profile of v0, /device:TPU:0, one launch (start us, length us, event | category | flops | bytes accessed | tf_op | source)
XLA Modules:
  0.0 82.8 jit_solution(17054151706888718566)
XLA Ops:
  0.0 6.1 %shard_map.64 = (bf16[4,144,512]{2,1,0:T(8,128)(2,1)}, bf16[4,144,512]{2,1,0:T(8,128)(2,1)}, bf16[4,144,256]{2,1,0:T(8,128)(2,1)}, bf16[4,144,256]{2,1,0:T(8,128...) custom-call(s32[1]{0:T(128)} %bitcast.place.refs_0_, s32[16]{0:T(128)} %mid.7, s32[16]{0:T(128)} %top.7, ...), custom_call_target="tpu_custom_call" | custom-call | tf_op jit(solution)/shard_map/pallas_call | solution.py:443
  6.1 0.0 copy-start.5
  6.2 0.0 copy-start.6
  6.2 0.5 collective-permute-start.2
  6.7 2.6 %collective-permute-start = (bf16[4,144,256]{2,1,0:T(8,128)(2,1)}, bf16[4,144,256]{2,1,0:T(8,128)(2,1)S(1)}, u32[]{:S(2)}, u32[]{:S(2)}) collective-permute-start(bf16[4,144,256]{2,1,0:T(8,128)(2,1)} %get-tuple-element.37), channel_id=1, source_target_pairs={{0,2},{1,3},{2,0},{3,1},{4,6},{5,7},{6,4},{7,5},{8,10},{9,11},{10,... | collective-permute-start | bytes 884744 | tf_op jit(solution)/shard_map/ppermute | solution.py:461
  9.3 0.1 collective-permute-start.1
  9.3 1.1 %copy-done = bf16[4,144,512]{2,1,0:T(8,128)(2,1)S(1)} copy-done((bf16[4,144,512]{2,1,0:T(8,128)(2,1)S(1)}, bf16[4,144,512]{2,1,0:T(8,128)(2,1)}, u32[]{:S(2)}) %copy-start) | copy-done | bytes 589848
  10.4 2.2 %collective-permute-start.3 = (bf16[2,144,256]{2,1,0:T(8,128)(2,1)S(1)}, bf16[2,144,256]{2,1,0:T(8,128)(2,1)S(1)}, u32[]{:S(2)}, u32[]{:S(2)}) collective-permute-start(bf16[2,144,256]{2,1,0:T(8,128)(2,1)S(1)} %get-tuple-element.44), channel_id=1, source_target_pairs={{0,4},{1,5},{2,6},{3,7},{4,0},{5,1},{6,2},{7,3},{8,12},{9,13},{10,... | collective-permute-start | bytes 442376 | tf_op jit(solution)/shard_map/ppermute | solution.py:461
  12.6 2.6 %collective-permute-start.4 = (bf16[2,144,256]{2,1,0:T(8,128)(2,1)S(1)}, bf16[2,144,256]{2,1,0:T(8,128)(2,1)S(1)}, u32[]{:S(2)}, u32[]{:S(2)}) collective-permute-start(bf16[2,144,256]{2,1,0:T(8,128)(2,1)S(1)} %get-tuple-element.45), channel_id=1, source_target_pairs={{0,8},{1,9},{2,10},{3,11},{4,12},{5,13},{6,14},{7,15},{8,0},{9,1},... | collective-permute-start | bytes 442376 | tf_op jit(solution)/shard_map/ppermute | solution.py:461
  15.3 6.8 %shard_map.65 = (f32[4,4,64,256]{3,2,1,0:T(8,128)S(1)}, f32[4,4,8,256]{3,2,1,0:T(8,128)S(1)}) custom-call(s32[1]{0:T(128)} %bitcast.place.refs_0_, s32[16]{0:T(128)S(1)} %copy-done.5, s32[16]{0:T(128)S(1)} %copy-done.6, bf16[4,144,512]{2,1,0:T(8,128)(2,1)S(1)} %copy-done.1, bf16[4,144,512]{2,1,0:T(8,128)(2,1)S(1)} %collective-permute-done.2.refs_1_.b_ref.refs_4_.refs_6_), custom_call_target="tpu_custom_call" | custom-call | tf_op jit(solution)/shard_map/pallas_call | solution.py:443
  22.1 1.1 %collective-permute-done.1.refs_1_.refs_3_.refs_6_ = bf16[4,144,256]{2,1,0:T(8,128)(2,1)S(1)} collective-permute-done((bf16[4,144,256]{2,1,0:T(8,128)(2,1)}, bf16[4,144,256]{2,1,0:T(8,128)(2,1)S(1)}, u32[]{:S(2)}, u32[]{:S(2)}) %collective-permute-start.1) | collective-permute-done | bytes 294944 | tf_op jit(solution)/shard_map/ppermute | solution.py:461
  23.1 3.5 %collective-permute-done.4.refs_6_.refs_9_ = bf16[2,144,256]{2,1,0:T(8,128)(2,1)S(1)} collective-permute-done((bf16[2,144,256]{2,1,0:T(8,128)(2,1)S(1)}, bf16[2,144,256]{2,1,0:T(8,128)(2,1)S(1)}, u32[]{:S(2)}, u32[]{:S(2)}) %collective-permute-start.4) | collective-permute-done | bytes 147488 | tf_op jit(solution)/shard_map/ppermute | solution.py:461
  26.7 1.6 %collective-permute-start.6 = (bf16[4,144,256]{2,1,0:T(8,128)(2,1)S(1)}, bf16[4,144,256]{2,1,0:T(8,128)(2,1)S(1)}, u32[]{:S(2)}, u32[]{:S(2)}) collective-permute-start(bf16[4,144,256]{2,1,0:T(8,128)(2,1)S(1)} %get-tuple-element.47), channel_id=1, source_target_pairs={{0,2},{1,3},{2,0},{3,1},{4,6},{5,7},{6,4},{7,5},{8,10},{9,11},{10,... | collective-permute-start | bytes 884744 | tf_op jit(solution)/shard_map/ppermute | solution.py:461
  28.2 2.4 %collective-permute-start.10 = (bf16[2,144,256]{2,1,0:T(8,128)(2,1)S(1)}, bf16[2,144,256]{2,1,0:T(8,128)(2,1)S(1)}, u32[]{:S(2)}, u32[]{:S(2)}) collective-permute-start(bf16[2,144,256]{2,1,0:T(8,128)(2,1)S(1)} %get-tuple-element.56), channel_id=1, source_target_pairs={{0,12},{1,13},{2,14},{3,15},{4,8},{5,9},{6,10},{7,11},{8,4},{9,5},... | collective-permute-start | bytes 442376 | tf_op jit(solution)/shard_map/ppermute | solution.py:461
  30.7 1.8 %collective-permute-start.8 = (bf16[2,144,256]{2,1,0:T(8,128)(2,1)S(1)}, bf16[2,144,256]{2,1,0:T(8,128)(2,1)S(1)}, u32[]{:S(2)}, u32[]{:S(2)}) collective-permute-start(bf16[2,144,256]{2,1,0:T(8,128)(2,1)S(1)} %get-tuple-element.54), channel_id=1, source_target_pairs={{0,4},{1,5},{2,6},{3,7},{4,0},{5,1},{6,2},{7,3},{8,12},{9,13},{10,... | collective-permute-start | bytes 442376 | tf_op jit(solution)/shard_map/ppermute | solution.py:461
  32.4 0.2 collective-permute-start.9
  32.6 8.1 %shard_map.68 = (f32[4,4,64,256]{3,2,1,0:T(8,128)S(1)}, f32[4,4,8,256]{3,2,1,0:T(8,128)S(1)}, f32[4,2,64,256]{3,2,1,0:T(8,128)S(1)}, f32[4,2,8,256]{3,2,1,0:T(8,128)S(1)}) custom-call(s32[1]{0:T(128)} %bitcast.place.refs_0_, s32[16]{0:T(128)S(1)} %copy-done.5, s32[16]{0:T(128)S(1)} %copy-done.6, bf16[4,144,512]{2,1,0:T(8,128)(2,1)S(1)} %copy-done.1, ...), custom_call_target="tpu_custom_call" | custom-call | tf_op jit(solution)/shard_map/pallas_call | solution.py:443
  40.7 5.2 %collective-permute-done.9.refs_10_ = bf16[2,144,256]{2,1,0:T(8,128)(2,1)S(1)} collective-permute-done((bf16[2,144,256]{2,1,0:T(8,128)(2,1)S(1)}, bf16[2,144,256]{2,1,0:T(8,128)(2,1)S(1)}, u32[]{:S(2)}, u32[]{:S(2)}) %collective-permute-start.9) | collective-permute-done | bytes 147488 | tf_op jit(solution)/shard_map/ppermute | solution.py:461
  45.9 8.0 %shard_map.69 = (bf16[64,1024]{1,0:T(8,128)(2,1)S(1)}, bf16[64,1024]{1,0:T(8,128)(2,1)S(1)}, bf16[64,1024]{1,0:T(8,128)(2,1)S(1)}, bf16[64,1024]{1,0:T(8,128)(2,1)S(1)}) custom-call(s32[1]{0:T(128)} %bitcast.place.refs_0_, s32[16]{0:T(128)S(1)} %copy-done.5, s32[16]{0:T(128)S(1)} %copy-done.6, bf16[4,144,512]{2,1,0:T(8,128)(2,1)S(1)} %copy-done.1, ...), custom_call_target="tpu_custom_call" | custom-call | tf_op jit(solution)/shard_map/pallas_call | solution.py:443
  53.9 0.1 collective-permute-start.11
  54.0 3.0 %collective-permute-start.12 = (bf16[64,1024]{1,0:T(8,128)(2,1)S(1)}, bf16[64,1024]{1,0:T(8,128)(2,1)S(1)}, u32[]{:S(2)}, u32[]{:S(2)}) collective-permute-start(bf16[64,1024]{1,0:T(8,128)(2,1)S(1)} %get-tuple-element.61), channel_id=1, source_target_pairs={{0,8},{1,9},{2,10},{3,11},{4,12},{5,13},{6,14},{7,15},{8,0},{9,1},... | collective-permute-start | bytes 393224 | tf_op jit(solution)/shard_map/ppermute | solution.py:461
  57.0 1.4 %collective-permute-start.13 = (bf16[64,1024]{1,0:T(8,128)(2,1)S(1)}, bf16[64,1024]{1,0:T(8,128)(2,1)S(1)}, u32[]{:S(2)}, u32[]{:S(2)}) collective-permute-start(bf16[64,1024]{1,0:T(8,128)(2,1)S(1)} %get-tuple-element.62), channel_id=1, source_target_pairs={{0,12},{1,13},{2,14},{3,15},{4,8},{5,9},{6,10},{7,11},{8,4},{9,5},... | collective-permute-start | bytes 393224 | tf_op jit(solution)/shard_map/ppermute | solution.py:461
  58.4 8.6 %shard_map.70 = (f32[4,4,64,256]{3,2,1,0:T(8,128)S(1)}, f32[4,4,8,256]{3,2,1,0:T(8,128)S(1)}) custom-call(s32[1]{0:T(128)} %bitcast.place.refs_0_, s32[16]{0:T(128)S(1)} %copy-done.5, s32[16]{0:T(128)S(1)} %copy-done.6, bf16[4,144,512]{2,1,0:T(8,128)(2,1)S(1)} %copy-done.1, bf16[4,144,512]{2,1,0:T(8,128)(2,1)S(1)} %collective-permute-done.2.refs_1_.b_ref.refs_4_.refs_6_, ...), custom_call_target="tpu_custom_call" | custom-call | tf_op jit(solution)/shard_map/pallas_call | solution.py:443
  67.0 0.1 shard_map.71
  67.2 0.9 %collective-permute-start.15 = (bf16[4,48,512]{2,1,0:T(8,128)(2,1)S(1)}, bf16[4,48,512]{2,1,0:T(8,128)(2,1)S(1)}, u32[]{:S(2)}, u32[]{:S(2)}) collective-permute-start(bf16[4,48,512]{2,1,0:T(8,128)(2,1)S(1)} %get-tuple-element.63.refs_9_), channel_id=1, source_target_pairs={{0,2},{1,3},{2,0},{3,1},{4,6},{5,7},{6,4},{7,5},{8,10},{9,11},{10,... | collective-permute-start | bytes 589832 | tf_op jit(solution)/shard_map/ppermute | solution.py:461
  68.0 4.8 %shard_map.72 = (f32[4,4,64,256]{3,2,1,0:T(8,128)S(1)}, f32[4,4,8,256]{3,2,1,0:T(8,128)S(1)}) custom-call(s32[1]{0:T(128)} %bitcast.place.refs_0_, s32[16]{0:T(128)S(1)} %copy-done.5, s32[16]{0:T(128)S(1)} %copy-done.6, bf16[4,144,256]{2,1,0:T(8,128)(2,1)S(1)} %collective-permute-done.6.refs_7_.refs_3_, ...), custom_call_target="tpu_custom_call" | custom-call | tf_op jit(solution)/shard_map/pallas_call | solution.py:443
  72.9 0.1 shard_map.73
  73.0 0.1 collective-permute-start.14
  73.1 1.3 %collective-permute-start.16 = (bf16[4,48,512]{2,1,0:T(8,128)(2,1)S(1)}, bf16[4,48,512]{2,1,0:T(8,128)(2,1)S(1)}, u32[]{:S(2)}, u32[]{:S(2)}) collective-permute-start(bf16[4,48,512]{2,1,0:T(8,128)(2,1)S(1)} %get-tuple-element.68), channel_id=1, source_target_pairs={{0,3},{1,2},{2,1},{3,0},{4,7},{5,6},{6,5},{7,4},{8,11},{9,10},{10,... | collective-permute-start | bytes 589832 | tf_op jit(solution)/shard_map/ppermute | solution.py:461
  74.4 0.1 collective-permute-done.14.refs_1_
  74.5 5.3 %collective-permute-done.16.refs_3_ = bf16[4,48,512]{2,1,0:T(8,128)(2,1)S(1)} collective-permute-done((bf16[4,48,512]{2,1,0:T(8,128)(2,1)S(1)}, bf16[4,48,512]{2,1,0:T(8,128)(2,1)S(1)}, u32[]{:S(2)}, u32[]{:S(2)}) %collective-permute-start.16) | collective-permute-done | bytes 196640 | tf_op jit(solution)/shard_map/ppermute | solution.py:461
  79.8 3.0 %shard_map.74 = bf16[512,768]{1,0:T(8,128)(2,1)} custom-call(s32[1]{0:T(128)} %bitcast.place.refs_0_, s32[16]{0:T(128)S(1)} %copy-done.5, s32[16]{0:T(128)S(1)} %copy-done.6, bf16[4,48,512]{2,1,0:T(8,128)(2,1)S(1)} %get-tuple-element.66.refs_0_, bf16[4,48,512]{2,1,0:T(8,128)(2,1)S(1)} %collective-permute-done.14.refs_1_, ...), custom_call_target="tpu_custom_call" | custom-call | tf_op jit(solution)/shard_map/pallas_call | solution.py:443
  (27 shorter events, 0.1 us)
Async XLA Ops:
  6.1 9.1 %copy-start.5 = (s32[16]{0:T(128)S(1)}, s32[16]{0:T(128)}, u32[]{:S(2)}) copy-start(s32[16]{0:T(128)} %mid.7) | copy-start | bytes 196
  6.2 9.1 %copy-start.6 = (s32[16]{0:T(128)S(1)}, s32[16]{0:T(128)}, u32[]{:S(2)}) copy-start(s32[16]{0:T(128)} %top.7) | copy-start | bytes 196
  6.2 3.2 %collective-permute-start.2 = (bf16[4,144,512]{2,1,0:T(8,128)(2,1)}, bf16[4,144,512]{2,1,0:T(8,128)(2,1)S(1)}, u32[]{:S(2)}, u32[]{:S(2)}) collective-permute-start(bf16[4,144,512]{2,1,0:T(8,128)(2,1)} %get-tuple-element.42), channel_id=1, source_target_pairs={{0,1},{1,0},{2,3},{3,2},{4,5},{5,4},{6,7},{7,6},{8,9},{9,8},{10,11... | collective-permute-start | bytes 1769480 | tf_op jit(solution)/shard_map/ppermute | solution.py:461
  6.7 15.4 %collective-permute-start = (bf16[4,144,256]{2,1,0:T(8,128)(2,1)}, bf16[4,144,256]{2,1,0:T(8,128)(2,1)S(1)}, u32[]{:S(2)}, u32[]{:S(2)}) collective-permute-start(bf16[4,144,256]{2,1,0:T(8,128)(2,1)} %get-tuple-element.37), channel_id=1, source_target_pairs={{0,2},{1,3},{2,0},{3,1},{4,6},{5,7},{6,4},{7,5},{8,10},{9,11},{10,... | collective-permute-start | bytes 884744 | tf_op jit(solution)/shard_map/ppermute | solution.py:461
  9.3 13.9 %collective-permute-start.1 = (bf16[4,144,256]{2,1,0:T(8,128)(2,1)}, bf16[4,144,256]{2,1,0:T(8,128)(2,1)S(1)}, u32[]{:S(2)}, u32[]{:S(2)}) collective-permute-start(bf16[4,144,256]{2,1,0:T(8,128)(2,1)} %get-tuple-element.38), channel_id=1, source_target_pairs={{0,3},{1,2},{2,1},{3,0},{4,7},{5,6},{6,5},{7,4},{8,11},{9,10},{10,... | collective-permute-start | bytes 884744 | tf_op jit(solution)/shard_map/ppermute | solution.py:461
  9.3 1.1 %copy-start = (bf16[4,144,512]{2,1,0:T(8,128)(2,1)S(1)}, bf16[4,144,512]{2,1,0:T(8,128)(2,1)}, u32[]{:S(2)}) copy-start(bf16[4,144,512]{2,1,0:T(8,128)(2,1)} %get-tuple-element.41.refs_0_.a_ref.refs_3_.refs_5_) | copy-start | bytes 1769476
  10.4 4.9 %copy-start.1 = (bf16[4,144,512]{2,1,0:T(8,128)(2,1)S(1)}, bf16[4,144,512]{2,1,0:T(8,128)(2,1)}, u32[]{:S(2)}) copy-start(bf16[4,144,512]{2,1,0:T(8,128)(2,1)} %get-tuple-element.41.refs_0_.a_ref.refs_3_.refs_5_) | copy-start | bytes 1769476
  10.4 16.2 %copy-start.3 = (bf16[4,144,256]{2,1,0:T(8,128)(2,1)S(1)}, bf16[4,144,256]{2,1,0:T(8,128)(2,1)}, u32[]{:S(2)}) copy-start(bf16[4,144,256]{2,1,0:T(8,128)(2,1)} %get-tuple-element.39.refs_2_) | copy-start | bytes 884740
  10.4 16.2 %copy-start.4 = (bf16[4,144,256]{2,1,0:T(8,128)(2,1)S(1)}, bf16[4,144,256]{2,1,0:T(8,128)(2,1)}, u32[]{:S(2)}) copy-start(bf16[4,144,256]{2,1,0:T(8,128)(2,1)} %get-tuple-element.40.refs_3_) | copy-start | bytes 884740
  10.4 12.7 %collective-permute-start.3 = (bf16[2,144,256]{2,1,0:T(8,128)(2,1)S(1)}, bf16[2,144,256]{2,1,0:T(8,128)(2,1)S(1)}, u32[]{:S(2)}, u32[]{:S(2)}) collective-permute-start(bf16[2,144,256]{2,1,0:T(8,128)(2,1)S(1)} %get-tuple-element.44), channel_id=1, source_target_pairs={{0,4},{1,5},{2,6},{3,7},{4,0},{5,1},{6,2},{7,3},{8,12},{9,13},{10,... | collective-permute-start | bytes 442376 | tf_op jit(solution)/shard_map/ppermute | solution.py:461
  12.6 14.0 %collective-permute-start.4 = (bf16[2,144,256]{2,1,0:T(8,128)(2,1)S(1)}, bf16[2,144,256]{2,1,0:T(8,128)(2,1)S(1)}, u32[]{:S(2)}, u32[]{:S(2)}) collective-permute-start(bf16[2,144,256]{2,1,0:T(8,128)(2,1)S(1)} %get-tuple-element.45), channel_id=1, source_target_pairs={{0,8},{1,9},{2,10},{3,11},{4,12},{5,13},{6,14},{7,15},{8,0},{9,1},... | collective-permute-start | bytes 442376 | tf_op jit(solution)/shard_map/ppermute | solution.py:461
  15.2 11.4 %collective-permute-start.5 = (bf16[2,144,256]{2,1,0:T(8,128)(2,1)S(1)}, bf16[2,144,256]{2,1,0:T(8,128)(2,1)S(1)}, u32[]{:S(2)}, u32[]{:S(2)}) collective-permute-start(bf16[2,144,256]{2,1,0:T(8,128)(2,1)S(1)} %get-tuple-element.46), channel_id=1, source_target_pairs={{0,12},{1,13},{2,14},{3,15},{4,8},{5,9},{6,10},{7,11},{8,4},{9,5},... | collective-permute-start | bytes 442376 | tf_op jit(solution)/shard_map/ppermute | solution.py:461
  26.7 31.7 %collective-permute-start.6 = (bf16[4,144,256]{2,1,0:T(8,128)(2,1)S(1)}, bf16[4,144,256]{2,1,0:T(8,128)(2,1)S(1)}, u32[]{:S(2)}, u32[]{:S(2)}) collective-permute-start(bf16[4,144,256]{2,1,0:T(8,128)(2,1)S(1)} %get-tuple-element.47), channel_id=1, source_target_pairs={{0,2},{1,3},{2,0},{3,1},{4,6},{5,7},{6,4},{7,5},{8,10},{9,11},{10,... | collective-permute-start | bytes 884744 | tf_op jit(solution)/shard_map/ppermute | solution.py:461
  28.2 30.2 %collective-permute-start.7 = (bf16[4,144,256]{2,1,0:T(8,128)(2,1)S(1)}, bf16[4,144,256]{2,1,0:T(8,128)(2,1)S(1)}, u32[]{:S(2)}, u32[]{:S(2)}) collective-permute-start(bf16[4,144,256]{2,1,0:T(8,128)(2,1)S(1)} %get-tuple-element.48), channel_id=1, source_target_pairs={{0,3},{1,2},{2,1},{3,0},{4,7},{5,6},{6,5},{7,4},{8,11},{9,10},{10,... | collective-permute-start | bytes 884744 | tf_op jit(solution)/shard_map/ppermute | solution.py:461
  28.2 12.5 %collective-permute-start.10 = (bf16[2,144,256]{2,1,0:T(8,128)(2,1)S(1)}, bf16[2,144,256]{2,1,0:T(8,128)(2,1)S(1)}, u32[]{:S(2)}, u32[]{:S(2)}) collective-permute-start(bf16[2,144,256]{2,1,0:T(8,128)(2,1)S(1)} %get-tuple-element.56), channel_id=1, source_target_pairs={{0,12},{1,13},{2,14},{3,15},{4,8},{5,9},{6,10},{7,11},{8,4},{9,5},... | collective-permute-start | bytes 442376 | tf_op jit(solution)/shard_map/ppermute | solution.py:461
  30.7 10.1 %collective-permute-start.8 = (bf16[2,144,256]{2,1,0:T(8,128)(2,1)S(1)}, bf16[2,144,256]{2,1,0:T(8,128)(2,1)S(1)}, u32[]{:S(2)}, u32[]{:S(2)}) collective-permute-start(bf16[2,144,256]{2,1,0:T(8,128)(2,1)S(1)} %get-tuple-element.54), channel_id=1, source_target_pairs={{0,4},{1,5},{2,6},{3,7},{4,0},{5,1},{6,2},{7,3},{8,12},{9,13},{10,... | collective-permute-start | bytes 442376 | tf_op jit(solution)/shard_map/ppermute | solution.py:461
  32.4 13.5 %collective-permute-start.9 = (bf16[2,144,256]{2,1,0:T(8,128)(2,1)S(1)}, bf16[2,144,256]{2,1,0:T(8,128)(2,1)S(1)}, u32[]{:S(2)}, u32[]{:S(2)}) collective-permute-start(bf16[2,144,256]{2,1,0:T(8,128)(2,1)S(1)} %get-tuple-element.55), channel_id=1, source_target_pairs={{0,8},{1,9},{2,10},{3,11},{4,12},{5,13},{6,14},{7,15},{8,0},{9,1},... | collective-permute-start | bytes 442376 | tf_op jit(solution)/shard_map/ppermute | solution.py:461
  53.9 13.1 %collective-permute-start.11 = (bf16[64,1024]{1,0:T(8,128)(2,1)S(1)}, bf16[64,1024]{1,0:T(8,128)(2,1)S(1)}, u32[]{:S(2)}, u32[]{:S(2)}) collective-permute-start(bf16[64,1024]{1,0:T(8,128)(2,1)S(1)} %get-tuple-element.60), channel_id=1, source_target_pairs={{0,4},{1,5},{2,6},{3,7},{4,0},{5,1},{6,2},{7,3},{8,12},{9,13},{10,... | collective-permute-start | bytes 393224 | tf_op jit(solution)/shard_map/ppermute | solution.py:461
  54.0 13.0 %collective-permute-start.12 = (bf16[64,1024]{1,0:T(8,128)(2,1)S(1)}, bf16[64,1024]{1,0:T(8,128)(2,1)S(1)}, u32[]{:S(2)}, u32[]{:S(2)}) collective-permute-start(bf16[64,1024]{1,0:T(8,128)(2,1)S(1)} %get-tuple-element.61), channel_id=1, source_target_pairs={{0,8},{1,9},{2,10},{3,11},{4,12},{5,13},{6,14},{7,15},{8,0},{9,1},... | collective-permute-start | bytes 393224 | tf_op jit(solution)/shard_map/ppermute | solution.py:461
  57.0 10.0 %collective-permute-start.13 = (bf16[64,1024]{1,0:T(8,128)(2,1)S(1)}, bf16[64,1024]{1,0:T(8,128)(2,1)S(1)}, u32[]{:S(2)}, u32[]{:S(2)}) collective-permute-start(bf16[64,1024]{1,0:T(8,128)(2,1)S(1)} %get-tuple-element.62), channel_id=1, source_target_pairs={{0,12},{1,13},{2,14},{3,15},{4,8},{5,9},{6,10},{7,11},{8,4},{9,5},... | collective-permute-start | bytes 393224 | tf_op jit(solution)/shard_map/ppermute | solution.py:461
  67.2 7.3 %collective-permute-start.15 = (bf16[4,48,512]{2,1,0:T(8,128)(2,1)S(1)}, bf16[4,48,512]{2,1,0:T(8,128)(2,1)S(1)}, u32[]{:S(2)}, u32[]{:S(2)}) collective-permute-start(bf16[4,48,512]{2,1,0:T(8,128)(2,1)S(1)} %get-tuple-element.63.refs_9_), channel_id=1, source_target_pairs={{0,2},{1,3},{2,0},{3,1},{4,6},{5,7},{6,4},{7,5},{8,10},{9,11},{10,... | collective-permute-start | bytes 589832 | tf_op jit(solution)/shard_map/ppermute | solution.py:461
  72.9 6.9 %copy-start.2 = (bf16[768,768]{1,0:T(8,128)(2,1)S(1)}, bf16[768,768]{1,0:T(8,128)(2,1)}, u32[]{:S(2)}) copy-start(bf16[768,768]{1,0:T(8,128)(2,1)} %refs_4_.1) | copy-start | bytes 3538948
  73.0 1.5 %collective-permute-start.14 = (bf16[4,48,512]{2,1,0:T(8,128)(2,1)S(1)}, bf16[4,48,512]{2,1,0:T(8,128)(2,1)S(1)}, u32[]{:S(2)}, u32[]{:S(2)}) collective-permute-start(bf16[4,48,512]{2,1,0:T(8,128)(2,1)S(1)} %get-tuple-element.67), channel_id=1, source_target_pairs={{0,1},{1,0},{2,3},{3,2},{4,5},{5,4},{6,7},{7,6},{8,9},{9,8},{10,11... | collective-permute-start | bytes 589832 | tf_op jit(solution)/shard_map/ppermute | solution.py:461
  73.1 6.7 %collective-permute-start.16 = (bf16[4,48,512]{2,1,0:T(8,128)(2,1)S(1)}, bf16[4,48,512]{2,1,0:T(8,128)(2,1)S(1)}, u32[]{:S(2)}, u32[]{:S(2)}) collective-permute-start(bf16[4,48,512]{2,1,0:T(8,128)(2,1)S(1)} %get-tuple-element.68), channel_id=1, source_target_pairs={{0,3},{1,2},{2,1},{3,0},{4,7},{5,6},{6,5},{7,4},{8,11},{9,10},{10,... | collective-permute-start | bytes 589832 | tf_op jit(solution)/shard_map/ppermute | solution.py:461
where the time goes:
time: 83 us; the launch traced here: 82.8 us
  Pallas kernels  45.8 us (55%)
  starting transfers between devices  20.6 us (25%)
  waiting for transfers between devices  15.1 us (18%)
  local copies, waits for them, and re-layouts  1.09 us (1%)
    pallas_call x11, Pallas kernels, call(): pl.pallas_call(body if after else kernel, grid_spec=pltpu.PrefetchScalarG...  45.8 us
    ppermute x17, starting transfers between devices, within(): return lax.ppermute(array, 'seq', [(i, i ^ apart) for i in range(count)])  20.6 us
    ppermute x17, waiting for transfers between devices, within(): return lax.ppermute(array, 'seq', [(i, i ^ apart) for i in range(count)])  15.1 us
  transfers between devices with their start and end apart: 17, of which 5 were waited for; matrix products, arithmetic and copies ran while one was open for 0% of the time, Pallas kernels for 44%

commit v1 on v0

--- a/solution.py
+++ b/solution.py
@@ -182,14 +182,9 @@
 
 
 def fill_class_major(block, picker, scratch):
-    ordered = dot(picker, block).astype(BF16)
-    step = 256
-    eye = (
-        lax.broadcasted_iota(jnp.int32, (step, step), 0)
-        == lax.broadcasted_iota(jnp.int32, (step, step), 1)
+    scratch[...] = lax.dot_general(
+        block, picker, (((0,), (1,)), ((), ())), preferred_element_type=F32
     ).astype(BF16)
-    for c in range(0, block.shape[1], step):
-        scratch[c : c + step, :] = dot_nt(eye, ordered[:, c : c + step]).astype(BF16)
 
 
 def lane_block(index):
@@ -330,7 +325,8 @@
 def far_kernel(place, mid, top, *refs):
     own, beyond = refs[:GROUP], refs[GROUP : GROUP + 6]
     outs = refs[GROUP + 6 : GROUP + 6 + RATE]
-    k_s, v_s = refs[GROUP + 6 + RATE :]
+    k_s, v_s, tail_s = refs[GROUP + 6 + RATE :]
+    tail_s[...] = jnp.zeros(tail_s.shape, F32)
     head = head_of(place, 0, 0)
     same = mid[head] == top[head]
     slots = (0, jnp.where(same, 0, 1))
@@ -346,7 +342,6 @@
                 k_s[level, s, here, :] = twice_keys(ref[0:DH, lane_block(slot)])
                 v_s[level, s, 0:DH, here] = ref[DH : 2 * DH, lane_block(slot)]
     v_s[:, :, DH:DX, :] = jnp.ones((2, RATE, DX - DH, TOK), BF16)
-    row = lax.broadcasted_iota(jnp.int32, (16, HALF), 0)
     tasks = [(s, level, chip) for s in range(RATE) for level in range(2) for chip in range(2)]
 
     def score(task):
@@ -378,49 +373,63 @@
         high = lse.astype(BF16).astype(F32)
         middle = (lse - high).astype(BF16).astype(F32)
         low = lse - high - middle
-        tail = jnp.where(row == 0, high, jnp.where(row == 1, middle, jnp.where(row == 2, low, 0.0)))
-        tail = tail.astype(BF16)
         for i in range(2):
-            start = (2 * chip + i) * HALF + level * BLK
-            lanes = slice(start, start + BLK)
-            outs[s][0:DH, lanes] = result[:, i * BLK : (i + 1) * BLK]
-            outs[s][DH:DX, lanes] = tail[:, i * BLK : (i + 1) * BLK]
+            n = 2 * (2 * chip + i) + level
+            outs[s][:, n * BLK : (n + 1) * BLK] = result[:, i * BLK : (i + 1) * BLK]
+            for k, part in enumerate((high, middle, low)):
+                tail_s[s, 3 * n + k : 3 * n + k + 1, :] = part[:, i * BLK : (i + 1) * BLK]
         scores = following
+    for s in range(RATE):
+        outs[s][:, GROUP * HALF :] = tail_s[s].astype(BF16)
+
+
+def join(acc, best, far, j):
+    tail = far[:, GROUP * HALF :].astype(F32)
+    lse = jnp.concatenate(
+        [
+            tail[3 * n : 3 * n + 1] + tail[3 * n + 1 : 3 * n + 2] + tail[3 * n + 2 : 3 * n + 3]
+            for n in (2 * j, 2 * j + 1)
+        ],
+        axis=1,
+    )
+    overall = jnp.maximum(best, lse)
+    near_factor, far_factor = jnp.exp2(best - overall), jnp.exp2(lse - overall)
+    total = acc[DH : DH + 1] * near_factor + far_factor
+    value = far[:, j * HALF : (j + 1) * HALF].astype(F32) * far_factor
+    return ((acc[0:DH] * near_factor + value) / total).astype(BF16)
 
 
 def combine_kernel(chip, acc_ref, max_ref, *refs):
     far, outs = refs[:HG], refs[HG:]
     for i in range(2):
-        lanes = slice((2 * chip + i) * HALF, (2 * chip + i + 1) * HALF)
         for p in range(HG):
-            acc, best = acc_ref[p, 2 * i], max_ref[p, 2 * i, 0:1, :]
-            tail = far[p][DH:DX, lanes].astype(F32)
-            lse = tail[0:1] + tail[1:2] + tail[2:3]
-            overall = jnp.maximum(best, lse)
-            near_factor, far_factor = jnp.exp2(best - overall), jnp.exp2(lse - overall)
-            total = acc[DH : DH + 1] * near_factor + far_factor
-            value = acc[0:DH] * near_factor + far[p][0:DH, lanes].astype(F32) * far_factor
-            outs[i][p, :, 0:HALF] = (value / total).astype(BF16)
+            outs[i][p, :, 0:HALF] = join(
+                acc_ref[p, 2 * i], max_ref[p, 2 * i, 0:1, :], far[p], 2 * chip + i
+            )
             acc = acc_ref[p, 2 * i + 1]
             outs[i][p, :, HALF:] = (acc[0:DH] / acc[DH : DH + 1]).astype(BF16)
 
 
 def project_kernel(place, mid, top, *refs):
     parts = refs[:GROUP]
-    w_ref, out_ref, held = refs[GROUP:]
-    for j in range(GROUP):
-        for p in range(HG):
-            head = head_of(place, j, p)
-            slots = class_of_slots(mid[head], top[head])
-            for s in range(RATE):
-                held[head_rows(head), lane_block(slots[s])] = parts[j][
-                    p, :, s * BLK : (s + 1) * BLK
-                ]
-    row = lax.broadcasted_iota(jnp.int32, (TOK, TOK), 0)
-    col = lax.broadcasted_iota(jnp.int32, (TOK, TOK), 1)
-    picker = (row == RATE * (col % BLK) + col // BLK).astype(BF16)
-    attention = dot_nt(picker, held[...]).astype(BF16)
-    out_ref[...] = dot(attention, w_ref[...]).astype(BF16)
+    w_ref, out_ref, held, attention = refs[GROUP:]
+
+    @pl.when(pl.program_id(0) == 0)
+    def _():
+        for j in range(GROUP):
+            for p in range(HG):
+                head = head_of(place, j, p)
+                slots = class_of_slots(mid[head], top[head])
+                for s in range(RATE):
+                    held[head_rows(head), lane_block(slots[s])] = parts[j][
+                        p, :, s * BLK : (s + 1) * BLK
+                    ]
+        row = lax.broadcasted_iota(jnp.int32, (TOK, TOK), 0)
+        col = lax.broadcasted_iota(jnp.int32, (TOK, TOK), 1)
+        picker = (row == RATE * (col % BLK) + col // BLK).astype(BF16)
+        attention[...] = dot_nt(picker, held[...]).astype(BF16)
+
+    out_ref[...] = dot(attention[...], w_ref[...]).astype(BF16)
 
 
 def whole(shape):
@@ -433,27 +442,32 @@
 
 def call(
     kernel, scalars, args, grid, in_specs, outs, scratch, scores,
-    limit=VMEM_LIMIT, aliases={}, after=(),
+    limit=VMEM_LIMIT, after=(), through=(),
 ):
     known = len(scalars) + len(args)
+    extra = (*after, *through)
+    count = len(outs)
+    anywhere = pl.BlockSpec(memory_space=pl.ANY)
 
     def body(*refs):
-        kernel(*refs[:known], *refs[known + len(after) :])
+        results = refs[known + len(extra) :]
+        kernel(*refs[:known], *results[:count], *results[count + len(through) :])
 
     return pl.pallas_call(
-        body if after else kernel,
+        body if extra else kernel,
         grid_spec=pltpu.PrefetchScalarGridSpec(
             num_scalar_prefetch=len(scalars),
             grid=grid,
-            in_specs=list(in_specs) + [pl.BlockSpec(memory_space=pl.ANY)] * len(after),
-            out_specs=[spec for spec, _ in outs],
+            in_specs=list(in_specs) + [anywhere] * len(extra),
+            out_specs=[spec for spec, _ in outs] + [anywhere] * len(through),
             scratch_shapes=scratch,
         ),
-        out_shape=[shape for _, shape in outs],
-        input_output_aliases=aliases,
+        out_shape=[shape for _, shape in outs]
+        + [jax.ShapeDtypeStruct(x.shape, x.dtype) for x in through],
+        input_output_aliases={known + len(after) + i: count + i for i in range(len(through))},
         compiler_params=pltpu.CompilerParams(vmem_limit_bytes=limit),
         cost_estimate=pl.CostEstimate(flops=0, bytes_accessed=0, transcendentals=0),
-    )(*scalars, *args, *after)
+    )(*scalars, *args, *extra)
 
 
 def within(array, apart):
@@ -487,14 +501,11 @@
     own1 = within(own1, 1)
     sel2, sel3 = within(sel2, 2), within(sel3, 3)
 
-    def regroup(a, b, through, after):
-        shapes = [jax.ShapeDtypeStruct(x.shape, x.dtype) for x in through] + [pair] * 3
+    def regroup(a, b, **order):
         return call(
-            regroup_kernel, (), (a, b, *through), (1,),
-            [whole(a.shape), whole(b.shape)] + [anywhere] * len(through),
-            [(anywhere, x) for x in shapes[: len(through)]] + [(whole(pair.shape), pair)] * 3,
-            [], 1 << 17,
-            aliases={2 + i: i for i in range(len(through))}, after=after,
+            regroup_kernel, (), (a, b), (1,),
+            [whole(a.shape), whole(b.shape)], [(whole(pair.shape), pair)] * 3,
+            [], 1 << 17, **order,
         )
 
     def state(count):
@@ -503,7 +514,7 @@
             for rows in (DX, 8)
         ]
 
-    def near(held, units, tasks, old, after=()):
+    def near(held, units, tasks, old, **order):
         sizes = [len(members) * BLK for _, members in units]
         scores = sum(sum(sizes[low:]) * HALF for group in tasks for _, low, _ in group)
         return call(
@@ -516,7 +527,7 @@
                 pltpu.VMEM((STEP, sum(sizes), 2 * DH), BF16),
                 pltpu.VMEM((STEP, DX, sum(sizes)), BF16),
             ],
-            HG * scores, after=after,
+            HG * scores, **order,
         )
 
     def units_of(a, b):
@@ -528,13 +539,11 @@
     other_sel, other_rest = units_of(2, 3)
     own = [(0, 0), (0, 1), (1, 0), (1, 1)]
 
-    ours = regroup(own0, own1, (), ())
+    ours = regroup(own0, own1)
     ours = [across(x, s + 1) for s, x in enumerate(ours)]
     held = {(0, 0): own0, (1, 0): own1}
     state_own = near(held, own_sel + own_rest, [[(q, 0, None) for q in own]], [])
-    rest2, rest3, *theirs = regroup(
-        sel2, sel3, (rest2, rest3), (state_own[1], *ours)
-    )
+    *theirs, rest2, rest3 = regroup(sel2, sel3, after=state_own[1:], through=(rest2, rest3))
     theirs = [across(x, s + 1) for s, x in enumerate(theirs)]
     rest2, rest3 = within(rest2, 2), within(rest3, 3)
     beyond = [x for both in zip(ours, theirs) for x in both]
@@ -547,10 +556,11 @@
             [((2, 0), 0, None), ((3, 0), 0, None)],
         ],
         [state_own],
+        after=ours,
     )
     state_own, state_sel = out[:2], out[2:]
 
-    result = jax.ShapeDtypeStruct((DX, GROUP * HALF), BF16)
+    result = jax.ShapeDtypeStruct((DH, GROUP * HALF + BLK), BF16)
     piece_0 = pl.BlockSpec((1, 3 * DH, HALF), lambda *_: (0, 0, 0))
     results = call(
         far_kernel, scalars, (own0, own1, sel2, sel3, *beyond), (1,),
@@ -559,6 +569,7 @@
         [
             pltpu.VMEM((2, RATE, TOK, 2 * DH), BF16),
             pltpu.VMEM((2, RATE, DX, TOK), BF16),
+            pltpu.VMEM((RATE, DH, BLK), F32),
         ],
         RATE * 2 * 3 * TOK * TOK, after=(out[1],),
     )
@@ -599,10 +610,15 @@
     part0, part1 = combine(0, state_own)
     parts = [part0, within(part1, 1), within(part2, 2), within(part3, 3)]
     return call(
-        project_kernel, scalars, (*parts, out_weight), (1,),
-        [whole(attended.shape)] * GROUP + [whole((width, width))],
-        [(whole((TOK, width)), jax.ShapeDtypeStruct((TOK, width), BF16))],
-        [pltpu.VMEM((width, TOK), BF16)],
+        project_kernel, scalars, (*parts, out_weight), (width // 256,),
+        [whole(attended.shape)] * GROUP + [pl.BlockSpec((width, 256), lambda n, *_: (0, n))],
+        [
+            (
+                pl.BlockSpec((TOK, 256), lambda n, *_: (0, n)),
+                jax.ShapeDtypeStruct((TOK, width), BF16),
+            )
+        ],
+        [pltpu.VMEM((width, TOK), BF16), pltpu.VMEM((TOK, width), BF16)],
         1 << 18,
     )[0]
 

time: 83 us -> 79.2 us (0.954)
  waiting for transfers between devices: 15.1 us -> 10.4 us
  starting transfers between devices: 20.6 us -> 21.8 us
    ppermute x17, waiting for transfers between devices: 15.1 us -> 10.4 us  [within(): return lax.ppermute(array, 'seq', [(i, i ^ apart) for i in range(count)])]
    ppermute x17, starting transfers between devices: 20.6 us -> 21.8 us  [within(): return lax.ppermute(array, 'seq', [(i, i ^ apart) for i in range(count)])]
  transfers between devices with their start and end apart: 17 -> 17, of which waited for: 5 -> 4; matrix products, arithmetic and copies ran while one was open for 0% -> 0% of each run, Pallas kernels for 44% -> 46%
where the time goes in v1:
time: 79.2 us; the launch traced here: 79 us
  Pallas kernels  45.5 us (57%)
  starting transfers between devices  21.8 us (28%)
  waiting for transfers between devices  10.4 us (13%)
  local copies, waits for them, and re-layouts  1.09 us (1%)
    pallas_call x11, Pallas kernels, call(): pl.pallas_call(body if extra else kernel, grid_spec=pltpu.PrefetchScalarG...  45.5 us
    ppermute x17, starting transfers between devices, within(): return lax.ppermute(array, 'seq', [(i, i ^ apart) for i in range(count)])  21.8 us
    ppermute x17, waiting for transfers between devices, within(): return lax.ppermute(array, 'seq', [(i, i ^ apart) for i in range(count)])  10.4 us
  transfers between devices with their start and end apart: 17, of which 4 were waited for; matrix products, arithmetic and copies ran while one was open for 0% of the time, Pallas kernels for 46%

profile of v1, /device:TPU:0, one launch (start us, length us, event | category | flops | bytes accessed | tf_op | source)
XLA Modules:
  0.0 79.0 jit_solution(17619937167489757851)
XLA Ops:
  0.0 5.3 %shard_map.64 = (bf16[4,144,512]{2,1,0:T(8,128)(2,1)}, bf16[4,144,512]{2,1,0:T(8,128)(2,1)}, bf16[4,144,256]{2,1,0:T(8,128)(2,1)}, bf16[4,144,256]{2,1,0:T(8,128...) custom-call(s32[1]{0:T(128)} %bitcast.place.refs_0_, s32[16]{0:T(128)} %mid.5, s32[16]{0:T(128)} %top.5, ...), custom_call_target="tpu_custom_call" | custom-call | tf_op jit(solution)/shard_map/pallas_call | solution.py:456
  5.3 0.0 copy-start.5
  5.3 0.0 copy-start.6
  5.3 0.5 collective-permute-start.2
  5.8 2.6 %collective-permute-start = (bf16[4,144,256]{2,1,0:T(8,128)(2,1)}, bf16[4,144,256]{2,1,0:T(8,128)(2,1)S(1)}, u32[]{:S(2)}, u32[]{:S(2)}) collective-permute-start(bf16[4,144,256]{2,1,0:T(8,128)(2,1)} %get-tuple-element.37), channel_id=1, source_target_pairs={{0,2},{1,3},{2,0},{3,1},{4,6},{5,7},{6,4},{7,5},{8,10},{9,11},{10,... | collective-permute-start | bytes 884744 | tf_op jit(solution)/shard_map/ppermute | solution.py:475
  8.4 0.1 collective-permute-start.1
  8.5 1.1 %copy-done = bf16[4,144,512]{2,1,0:T(8,128)(2,1)S(1)} copy-done((bf16[4,144,512]{2,1,0:T(8,128)(2,1)S(1)}, bf16[4,144,512]{2,1,0:T(8,128)(2,1)}, u32[]{:S(2)}) %copy-start) | copy-done | bytes 589848
  9.6 2.2 %collective-permute-start.5 = (bf16[2,144,256]{2,1,0:T(8,128)(2,1)S(1)}, bf16[2,144,256]{2,1,0:T(8,128)(2,1)S(1)}, u32[]{:S(2)}, u32[]{:S(2)}) collective-permute-start(bf16[2,144,256]{2,1,0:T(8,128)(2,1)S(1)} %get-tuple-element.47), channel_id=1, source_target_pairs={{0,4},{1,5},{2,6},{3,7},{4,0},{5,1},{6,2},{7,3},{8,12},{9,13},{10,... | collective-permute-start | bytes 442376 | tf_op jit(solution)/shard_map/ppermute | solution.py:475
  11.8 2.6 %collective-permute-start.6 = (bf16[2,144,256]{2,1,0:T(8,128)(2,1)S(1)}, bf16[2,144,256]{2,1,0:T(8,128)(2,1)S(1)}, u32[]{:S(2)}, u32[]{:S(2)}) collective-permute-start(bf16[2,144,256]{2,1,0:T(8,128)(2,1)S(1)} %get-tuple-element.48), channel_id=1, source_target_pairs={{0,8},{1,9},{2,10},{3,11},{4,12},{5,13},{6,14},{7,15},{8,0},{9,1},... | collective-permute-start | bytes 442376 | tf_op jit(solution)/shard_map/ppermute | solution.py:475
  14.4 6.8 %shard_map.65 = (f32[4,4,64,256]{3,2,1,0:T(8,128)S(1)}, f32[4,4,8,256]{3,2,1,0:T(8,128)S(1)}) custom-call(s32[1]{0:T(128)} %bitcast.place.refs_0_, s32[16]{0:T(128)S(1)} %copy-done.5, s32[16]{0:T(128)S(1)} %copy-done.6, bf16[4,144,512]{2,1,0:T(8,128)(2,1)S(1)} %copy-done.1, bf16[4,144,512]{2,1,0:T(8,128)(2,1)S(1)} %collective-permute-done.2.refs_1_.b_ref.refs_4_.refs_6_), custom_call_target="tpu_custom_call" | custom-call | tf_op jit(solution)/shard_map/pallas_call | solution.py:456
  21.2 1.1 %collective-permute-done.1.refs_1_.refs_6_ = bf16[4,144,256]{2,1,0:T(8,128)(2,1)S(1)} collective-permute-done((bf16[4,144,256]{2,1,0:T(8,128)(2,1)}, bf16[4,144,256]{2,1,0:T(8,128)(2,1)S(1)}, u32[]{:S(2)}, u32[]{:S(2)}) %collective-permute-start.1) | collective-permute-done | bytes 294944 | tf_op jit(solution)/shard_map/ppermute | solution.py:475
  22.3 1.6 %collective-permute-start.3 = (bf16[4,144,256]{2,1,0:T(8,128)(2,1)S(1)}, bf16[4,144,256]{2,1,0:T(8,128)(2,1)S(1)}, u32[]{:S(2)}, u32[]{:S(2)}) collective-permute-start(bf16[4,144,256]{2,1,0:T(8,128)(2,1)S(1)} %get-tuple-element.44), channel_id=1, source_target_pairs={{0,2},{1,3},{2,0},{3,1},{4,6},{5,7},{6,4},{7,5},{8,10},{9,11},{10,... | collective-permute-start | bytes 884744 | tf_op jit(solution)/shard_map/ppermute | solution.py:475
  23.9 0.3 collective-permute-start.4
  24.2 3.8 %collective-permute-start.10 = (bf16[2,144,256]{2,1,0:T(8,128)(2,1)S(1)}, bf16[2,144,256]{2,1,0:T(8,128)(2,1)S(1)}, u32[]{:S(2)}, u32[]{:S(2)}) collective-permute-start(bf16[2,144,256]{2,1,0:T(8,128)(2,1)S(1)} %get-tuple-element.56), channel_id=1, source_target_pairs={{0,12},{1,13},{2,14},{3,15},{4,8},{5,9},{6,10},{7,11},{8,4},{9,5},... | collective-permute-start | bytes 442376 | tf_op jit(solution)/shard_map/ppermute | solution.py:475
  28.0 1.4 %collective-permute-start.9 = (bf16[2,144,256]{2,1,0:T(8,128)(2,1)S(1)}, bf16[2,144,256]{2,1,0:T(8,128)(2,1)S(1)}, u32[]{:S(2)}, u32[]{:S(2)}) collective-permute-start(bf16[2,144,256]{2,1,0:T(8,128)(2,1)S(1)} %get-tuple-element.55), channel_id=1, source_target_pairs={{0,8},{1,9},{2,10},{3,11},{4,12},{5,13},{6,14},{7,15},{8,0},{9,1},... | collective-permute-start | bytes 442376 | tf_op jit(solution)/shard_map/ppermute | solution.py:475
  29.4 8.1 %shard_map.68 = (f32[4,4,64,256]{3,2,1,0:T(8,128)S(1)}, f32[4,4,8,256]{3,2,1,0:T(8,128)S(1)}, f32[4,2,64,256]{3,2,1,0:T(8,128)S(1)}, f32[4,2,8,256]{3,2,1,0:T(8,128)S(1)}) custom-call(s32[1]{0:T(128)} %bitcast.place.refs_0_, s32[16]{0:T(128)S(1)} %copy-done.5, s32[16]{0:T(128)S(1)} %copy-done.6, bf16[4,144,512]{2,1,0:T(8,128)(2,1)S(1)} %copy-done.1, ...), custom_call_target="tpu_custom_call" | custom-call | tf_op jit(solution)/shard_map/pallas_call | solution.py:456
  37.5 3.3 %collective-permute-done.9.refs_10_ = bf16[2,144,256]{2,1,0:T(8,128)(2,1)S(1)} collective-permute-done((bf16[2,144,256]{2,1,0:T(8,128)(2,1)S(1)}, bf16[2,144,256]{2,1,0:T(8,128)(2,1)S(1)}, u32[]{:S(2)}, u32[]{:S(2)}) %collective-permute-start.9) | collective-permute-done | bytes 147488 | tf_op jit(solution)/shard_map/ppermute | solution.py:475
  40.8 8.0 %shard_map.69 = (bf16[48,1152]{1,0:T(8,128)(2,1)S(1)}, bf16[48,1152]{1,0:T(8,128)(2,1)S(1)}, bf16[48,1152]{1,0:T(8,128)(2,1)S(1)}, bf16[48,1152]{1,0:T(8,128)(2,1)S(1)}) custom-call(s32[1]{0:T(128)} %bitcast.place.refs_0_, s32[16]{0:T(128)S(1)} %copy-done.5, s32[16]{0:T(128)S(1)} %copy-done.6, bf16[4,144,512]{2,1,0:T(8,128)(2,1)S(1)} %copy-done.1, ...), custom_call_target="tpu_custom_call" | custom-call | tf_op jit(solution)/shard_map/pallas_call | solution.py:456
  48.8 0.1 collective-permute-start.11
  48.9 3.0 %collective-permute-start.12 = (bf16[48,1152]{1,0:T(8,128)(2,1)S(1)}, bf16[48,1152]{1,0:T(8,128)(2,1)S(1)}, u32[]{:S(2)}, u32[]{:S(2)}) collective-permute-start(bf16[48,1152]{1,0:T(8,128)(2,1)S(1)} %get-tuple-element.61), channel_id=1, source_target_pairs={{0,8},{1,9},{2,10},{3,11},{4,12},{5,13},{6,14},{7,15},{8,0},{9,1},... | collective-permute-start | bytes 331784 | tf_op jit(solution)/shard_map/ppermute | solution.py:475
  51.9 1.3 %collective-permute-start.13 = (bf16[48,1152]{1,0:T(8,128)(2,1)S(1)}, bf16[48,1152]{1,0:T(8,128)(2,1)S(1)}, u32[]{:S(2)}, u32[]{:S(2)}) collective-permute-start(bf16[48,1152]{1,0:T(8,128)(2,1)S(1)} %get-tuple-element.62), channel_id=1, source_target_pairs={{0,12},{1,13},{2,14},{3,15},{4,8},{5,9},{6,10},{7,11},{8,4},{9,5},... | collective-permute-start | bytes 331784 | tf_op jit(solution)/shard_map/ppermute | solution.py:475
  53.3 8.6 %shard_map.70 = (f32[4,4,64,256]{3,2,1,0:T(8,128)S(1)}, f32[4,4,8,256]{3,2,1,0:T(8,128)S(1)}) custom-call(s32[1]{0:T(128)} %bitcast.place.refs_0_, s32[16]{0:T(128)S(1)} %copy-done.5, s32[16]{0:T(128)S(1)} %copy-done.6, bf16[4,144,512]{2,1,0:T(8,128)(2,1)S(1)} %copy-done.1, bf16[4,144,512]{2,1,0:T(8,128)(2,1)S(1)} %collective-permute-done.2.refs_1_.b_ref.refs_4_.refs_6_, ...), custom_call_target="tpu_custom_call" | custom-call | tf_op jit(solution)/shard_map/pallas_call | solution.py:456
  61.9 0.1 shard_map.71
  62.1 1.6 %collective-permute-start.15 = (bf16[4,48,512]{2,1,0:T(8,128)(2,1)S(1)}, bf16[4,48,512]{2,1,0:T(8,128)(2,1)S(1)}, u32[]{:S(2)}, u32[]{:S(2)}) collective-permute-start(bf16[4,48,512]{2,1,0:T(8,128)(2,1)S(1)} %get-tuple-element.63.refs_9_), channel_id=1, source_target_pairs={{0,2},{1,3},{2,0},{3,1},{4,6},{5,7},{6,4},{7,5},{8,10},{9,11},{10,... | collective-permute-start | bytes 589832 | tf_op jit(solution)/shard_map/ppermute | solution.py:475
  63.6 4.8 %shard_map.72 = (f32[4,4,64,256]{3,2,1,0:T(8,128)S(1)}, f32[4,4,8,256]{3,2,1,0:T(8,128)S(1)}) custom-call(s32[1]{0:T(128)} %bitcast.place.refs_0_, s32[16]{0:T(128)S(1)} %copy-done.5, s32[16]{0:T(128)S(1)} %copy-done.6, bf16[4,144,256]{2,1,0:T(8,128)(2,1)S(1)} %collective-permute-done.3.refs_7_.refs_3_, ...), custom_call_target="tpu_custom_call" | custom-call | tf_op jit(solution)/shard_map/pallas_call | solution.py:456
  68.4 0.0 copy-start.2
  68.4 0.2 shard_map.73
  68.6 0.1 collective-permute-start.14
  68.7 0.7 collective-permute-start.16
  69.3 0.8 collective-permute-done.14.refs_1_
  70.1 5.3 %collective-permute-done.16.refs_3_ = bf16[4,48,512]{2,1,0:T(8,128)(2,1)S(1)} collective-permute-done((bf16[4,48,512]{2,1,0:T(8,128)(2,1)S(1)}, bf16[4,48,512]{2,1,0:T(8,128)(2,1)S(1)}, u32[]{:S(2)}, u32[]{:S(2)}) %collective-permute-start.16) | collective-permute-done | bytes 196640 | tf_op jit(solution)/shard_map/ppermute | solution.py:475
  75.4 3.6 %shard_map.74 = bf16[512,768]{1,0:T(8,128)(2,1)} custom-call(s32[1]{0:T(128)} %bitcast.place.refs_0_, s32[16]{0:T(128)S(1)} %copy-done.5, s32[16]{0:T(128)S(1)} %copy-done.6, bf16[4,48,512]{2,1,0:T(8,128)(2,1)S(1)} %get-tuple-element.66.refs_0_, bf16[4,48,512]{2,1,0:T(8,128)(2,1)S(1)} %collective-permute-done.14.refs_1_, ...), custom_call_target="tpu_custom_call" | custom-call | tf_op jit(solution)/shard_map/pallas_call | solution.py:456
  (27 shorter events, 0.1 us)
Async XLA Ops:
  5.3 9.1 %copy-start.5 = (s32[16]{0:T(128)S(1)}, s32[16]{0:T(128)}, u32[]{:S(2)}) copy-start(s32[16]{0:T(128)} %mid.5) | copy-start | bytes 196
  5.3 9.1 %copy-start.6 = (s32[16]{0:T(128)S(1)}, s32[16]{0:T(128)}, u32[]{:S(2)}) copy-start(s32[16]{0:T(128)} %top.5) | copy-start | bytes 196
  5.3 3.2 %collective-permute-start.2 = (bf16[4,144,512]{2,1,0:T(8,128)(2,1)}, bf16[4,144,512]{2,1,0:T(8,128)(2,1)S(1)}, u32[]{:S(2)}, u32[]{:S(2)}) collective-permute-start(bf16[4,144,512]{2,1,0:T(8,128)(2,1)} %get-tuple-element.40), channel_id=1, source_target_pairs={{0,1},{1,0},{2,3},{3,2},{4,5},{5,4},{6,7},{7,6},{8,9},{9,8},{10,11... | collective-permute-start | bytes 1769480 | tf_op jit(solution)/shard_map/ppermute | solution.py:475
  5.8 15.4 %collective-permute-start = (bf16[4,144,256]{2,1,0:T(8,128)(2,1)}, bf16[4,144,256]{2,1,0:T(8,128)(2,1)S(1)}, u32[]{:S(2)}, u32[]{:S(2)}) collective-permute-start(bf16[4,144,256]{2,1,0:T(8,128)(2,1)} %get-tuple-element.37), channel_id=1, source_target_pairs={{0,2},{1,3},{2,0},{3,1},{4,6},{5,7},{6,4},{7,5},{8,10},{9,11},{10,... | collective-permute-start | bytes 884744 | tf_op jit(solution)/shard_map/ppermute | solution.py:475
  8.4 13.9 %collective-permute-start.1 = (bf16[4,144,256]{2,1,0:T(8,128)(2,1)}, bf16[4,144,256]{2,1,0:T(8,128)(2,1)S(1)}, u32[]{:S(2)}, u32[]{:S(2)}) collective-permute-start(bf16[4,144,256]{2,1,0:T(8,128)(2,1)} %get-tuple-element.38), channel_id=1, source_target_pairs={{0,3},{1,2},{2,1},{3,0},{4,7},{5,6},{6,5},{7,4},{8,11},{9,10},{10,... | collective-permute-start | bytes 884744 | tf_op jit(solution)/shard_map/ppermute | solution.py:475
  8.5 1.1 %copy-start = (bf16[4,144,512]{2,1,0:T(8,128)(2,1)S(1)}, bf16[4,144,512]{2,1,0:T(8,128)(2,1)}, u32[]{:S(2)}) copy-start(bf16[4,144,512]{2,1,0:T(8,128)(2,1)} %get-tuple-element.39.refs_0_.a_ref.refs_3_.refs_5_) | copy-start | bytes 1769476
  9.5 4.9 %copy-start.1 = (bf16[4,144,512]{2,1,0:T(8,128)(2,1)S(1)}, bf16[4,144,512]{2,1,0:T(8,128)(2,1)}, u32[]{:S(2)}) copy-start(bf16[4,144,512]{2,1,0:T(8,128)(2,1)} %get-tuple-element.39.refs_0_.a_ref.refs_3_.refs_5_) | copy-start | bytes 1769476
  9.5 12.7 %copy-start.3 = (bf16[4,144,256]{2,1,0:T(8,128)(2,1)S(1)}, bf16[4,144,256]{2,1,0:T(8,128)(2,1)}, u32[]{:S(2)}) copy-start(bf16[4,144,256]{2,1,0:T(8,128)(2,1)} %get-tuple-element.42.refs_3_) | copy-start | bytes 884740
  9.5 12.7 %copy-start.4 = (bf16[4,144,256]{2,1,0:T(8,128)(2,1)S(1)}, bf16[4,144,256]{2,1,0:T(8,128)(2,1)}, u32[]{:S(2)}) copy-start(bf16[4,144,256]{2,1,0:T(8,128)(2,1)} %get-tuple-element.43.refs_4_) | copy-start | bytes 884740
  9.6 14.6 %collective-permute-start.5 = (bf16[2,144,256]{2,1,0:T(8,128)(2,1)S(1)}, bf16[2,144,256]{2,1,0:T(8,128)(2,1)S(1)}, u32[]{:S(2)}, u32[]{:S(2)}) collective-permute-start(bf16[2,144,256]{2,1,0:T(8,128)(2,1)S(1)} %get-tuple-element.47), channel_id=1, source_target_pairs={{0,4},{1,5},{2,6},{3,7},{4,0},{5,1},{6,2},{7,3},{8,12},{9,13},{10,... | collective-permute-start | bytes 442376 | tf_op jit(solution)/shard_map/ppermute | solution.py:475
  11.8 16.2 %collective-permute-start.6 = (bf16[2,144,256]{2,1,0:T(8,128)(2,1)S(1)}, bf16[2,144,256]{2,1,0:T(8,128)(2,1)S(1)}, u32[]{:S(2)}, u32[]{:S(2)}) collective-permute-start(bf16[2,144,256]{2,1,0:T(8,128)(2,1)S(1)} %get-tuple-element.48), channel_id=1, source_target_pairs={{0,8},{1,9},{2,10},{3,11},{4,12},{5,13},{6,14},{7,15},{8,0},{9,1},... | collective-permute-start | bytes 442376 | tf_op jit(solution)/shard_map/ppermute | solution.py:475
  14.4 13.6 %collective-permute-start.7 = (bf16[2,144,256]{2,1,0:T(8,128)(2,1)S(1)}, bf16[2,144,256]{2,1,0:T(8,128)(2,1)S(1)}, u32[]{:S(2)}, u32[]{:S(2)}) collective-permute-start(bf16[2,144,256]{2,1,0:T(8,128)(2,1)S(1)} %get-tuple-element.49), channel_id=1, source_target_pairs={{0,12},{1,13},{2,14},{3,15},{4,8},{5,9},{6,10},{7,11},{8,4},{9,5},... | collective-permute-start | bytes 442376 | tf_op jit(solution)/shard_map/ppermute | solution.py:475
  22.3 31.0 %collective-permute-start.3 = (bf16[4,144,256]{2,1,0:T(8,128)(2,1)S(1)}, bf16[4,144,256]{2,1,0:T(8,128)(2,1)S(1)}, u32[]{:S(2)}, u32[]{:S(2)}) collective-permute-start(bf16[4,144,256]{2,1,0:T(8,128)(2,1)S(1)} %get-tuple-element.44), channel_id=1, source_target_pairs={{0,2},{1,3},{2,0},{3,1},{4,6},{5,7},{6,4},{7,5},{8,10},{9,11},{10,... | collective-permute-start | bytes 884744 | tf_op jit(solution)/shard_map/ppermute | solution.py:475
  23.9 29.4 %collective-permute-start.4 = (bf16[4,144,256]{2,1,0:T(8,128)(2,1)S(1)}, bf16[4,144,256]{2,1,0:T(8,128)(2,1)S(1)}, u32[]{:S(2)}, u32[]{:S(2)}) collective-permute-start(bf16[4,144,256]{2,1,0:T(8,128)(2,1)S(1)} %get-tuple-element.45), channel_id=1, source_target_pairs={{0,3},{1,2},{2,1},{3,0},{4,7},{5,6},{6,5},{7,4},{8,11},{9,10},{10,... | collective-permute-start | bytes 884744 | tf_op jit(solution)/shard_map/ppermute | solution.py:475
  24.2 13.3 %collective-permute-start.10 = (bf16[2,144,256]{2,1,0:T(8,128)(2,1)S(1)}, bf16[2,144,256]{2,1,0:T(8,128)(2,1)S(1)}, u32[]{:S(2)}, u32[]{:S(2)}) collective-permute-start(bf16[2,144,256]{2,1,0:T(8,128)(2,1)S(1)} %get-tuple-element.56), channel_id=1, source_target_pairs={{0,12},{1,13},{2,14},{3,15},{4,8},{5,9},{6,10},{7,11},{8,4},{9,5},... | collective-permute-start | bytes 442376 | tf_op jit(solution)/shard_map/ppermute | solution.py:475
  28.0 9.5 %collective-permute-start.8 = (bf16[2,144,256]{2,1,0:T(8,128)(2,1)S(1)}, bf16[2,144,256]{2,1,0:T(8,128)(2,1)S(1)}, u32[]{:S(2)}, u32[]{:S(2)}) collective-permute-start(bf16[2,144,256]{2,1,0:T(8,128)(2,1)S(1)} %get-tuple-element.54), channel_id=1, source_target_pairs={{0,4},{1,5},{2,6},{3,7},{4,0},{5,1},{6,2},{7,3},{8,12},{9,13},{10,... | collective-permute-start | bytes 442376 | tf_op jit(solution)/shard_map/ppermute | solution.py:475
  28.0 12.9 %collective-permute-start.9 = (bf16[2,144,256]{2,1,0:T(8,128)(2,1)S(1)}, bf16[2,144,256]{2,1,0:T(8,128)(2,1)S(1)}, u32[]{:S(2)}, u32[]{:S(2)}) collective-permute-start(bf16[2,144,256]{2,1,0:T(8,128)(2,1)S(1)} %get-tuple-element.55), channel_id=1, source_target_pairs={{0,8},{1,9},{2,10},{3,11},{4,12},{5,13},{6,14},{7,15},{8,0},{9,1},... | collective-permute-start | bytes 442376 | tf_op jit(solution)/shard_map/ppermute | solution.py:475
  48.8 13.1 %collective-permute-start.11 = (bf16[48,1152]{1,0:T(8,128)(2,1)S(1)}, bf16[48,1152]{1,0:T(8,128)(2,1)S(1)}, u32[]{:S(2)}, u32[]{:S(2)}) collective-permute-start(bf16[48,1152]{1,0:T(8,128)(2,1)S(1)} %get-tuple-element.60), channel_id=1, source_target_pairs={{0,4},{1,5},{2,6},{3,7},{4,0},{5,1},{6,2},{7,3},{8,12},{9,13},{10,... | collective-permute-start | bytes 331784 | tf_op jit(solution)/shard_map/ppermute | solution.py:475
  48.9 13.0 %collective-permute-start.12 = (bf16[48,1152]{1,0:T(8,128)(2,1)S(1)}, bf16[48,1152]{1,0:T(8,128)(2,1)S(1)}, u32[]{:S(2)}, u32[]{:S(2)}) collective-permute-start(bf16[48,1152]{1,0:T(8,128)(2,1)S(1)} %get-tuple-element.61), channel_id=1, source_target_pairs={{0,8},{1,9},{2,10},{3,11},{4,12},{5,13},{6,14},{7,15},{8,0},{9,1},... | collective-permute-start | bytes 331784 | tf_op jit(solution)/shard_map/ppermute | solution.py:475
  51.9 10.0 %collective-permute-start.13 = (bf16[48,1152]{1,0:T(8,128)(2,1)S(1)}, bf16[48,1152]{1,0:T(8,128)(2,1)S(1)}, u32[]{:S(2)}, u32[]{:S(2)}) collective-permute-start(bf16[48,1152]{1,0:T(8,128)(2,1)S(1)} %get-tuple-element.62), channel_id=1, source_target_pairs={{0,12},{1,13},{2,14},{3,15},{4,8},{5,9},{6,10},{7,11},{8,4},{9,5},... | collective-permute-start | bytes 331784 | tf_op jit(solution)/shard_map/ppermute | solution.py:475
  62.1 8.0 %collective-permute-start.15 = (bf16[4,48,512]{2,1,0:T(8,128)(2,1)S(1)}, bf16[4,48,512]{2,1,0:T(8,128)(2,1)S(1)}, u32[]{:S(2)}, u32[]{:S(2)}) collective-permute-start(bf16[4,48,512]{2,1,0:T(8,128)(2,1)S(1)} %get-tuple-element.63.refs_9_), channel_id=1, source_target_pairs={{0,2},{1,3},{2,0},{3,1},{4,6},{5,7},{6,4},{7,5},{8,10},{9,11},{10,... | collective-permute-start | bytes 589832 | tf_op jit(solution)/shard_map/ppermute | solution.py:475
  68.4 6.9 %copy-start.2 = (bf16[768,768]{1,0:T(8,128)(2,1)S(1)}, bf16[768,768]{1,0:T(8,128)(2,1)}, u32[]{:S(2)}) copy-start(bf16[768,768]{1,0:T(8,128)(2,1)} %refs_4_.1) | copy-start | bytes 3538948
  68.6 1.5 %collective-permute-start.14 = (bf16[4,48,512]{2,1,0:T(8,128)(2,1)S(1)}, bf16[4,48,512]{2,1,0:T(8,128)(2,1)S(1)}, u32[]{:S(2)}, u32[]{:S(2)}) collective-permute-start(bf16[4,48,512]{2,1,0:T(8,128)(2,1)S(1)} %get-tuple-element.67), channel_id=1, source_target_pairs={{0,1},{1,0},{2,3},{3,2},{4,5},{5,4},{6,7},{7,6},{8,9},{9,8},{10,11... | collective-permute-start | bytes 589832 | tf_op jit(solution)/shard_map/ppermute | solution.py:475
  68.7 6.7 %collective-permute-start.16 = (bf16[4,48,512]{2,1,0:T(8,128)(2,1)S(1)}, bf16[4,48,512]{2,1,0:T(8,128)(2,1)S(1)}, u32[]{:S(2)}, u32[]{:S(2)}) collective-permute-start(bf16[4,48,512]{2,1,0:T(8,128)(2,1)S(1)} %get-tuple-element.68), channel_id=1, source_target_pairs={{0,3},{1,2},{2,1},{3,0},{4,7},{5,6},{6,5},{7,4},{8,11},{9,10},{10,... | collective-permute-start | bytes 589832 | tf_op jit(solution)/shard_map/ppermute | solution.py:475
